TPU v7x, 256 devices: a whole 4x4x8 slice. The times are simulated.
256 devices in a mesh: blk: 64 (over x, y_hi, z), rep: 4 (over y_lo, core).
Axes of the slice: x: 4, y: 4 (y_hi: 2, y_lo: 2; y = y_hi * 2 + y_lo), z: 8, core: 2. Of those that a mesh axis runs over, the one named last changes fastest.
Arguments:
- features: bfloat16 [32768, 512], P('blk', 'rep'), may hold values from -6 to 6
- row_target: int32 [32768], P('blk'), may hold values from 0 to 32767, as said below
- tile_values: bfloat16 [64, 64, 4, 128, 128], P('blk'), may hold values from -0.25 to 0.25
- tile_rows: int32 [64, 64, 4], P('blk'), may hold values from 0 to 3, as said below
- tile_cols: int32 [64, 64, 4], P('blk'), may hold values from 0 to 3, as said below
- tile_counts: int32 [64, 64], P('blk'), may hold values from 0 to 4, as said below
- weight: bfloat16 [512, 512], P('rep'), may hold values from -0.25 to 0.25
- layer_bias: float32 [512], replicated, may hold values from -3 to 3
- out_grad: bfloat16 [32768, 512], P('blk'), may hold values from -0.75 to 0.75
Outputs:
- output: bfloat16 [32768, 512], P(('blk', 'rep'))
- weight_grad: float32 [512, 512], P('rep')
- bias_grad: float32 [512], replicated
- feature_grad: bfloat16 [32768, 512], P('blk', 'rep')
Inputs may be any that keep to these rules, and one draw needn't show every extreme that they name: `row_target`: a permutation of the 32768 rows; the rows of one loader block of 512 rows bound for one partition number at most 16, and this many in every draw. `tile_rows`: within one pair of partitions the live slots name distinct tile positions. `tile_cols`: within one pair of partitions the live slots name distinct tile positions. `tile_counts`: every pair of a partition with itself has all 4 slots live; each row partition has live slots with exactly 6 other partitions, and none with the rest.
All inputs are finite; a program needn't handle non-finite values.
Results may differ from a plain program's by a relative error of at most 0.0061.
Values may be sent and summed in bfloat16 or wider, within the bound.
A program may use at most 128 MiB of HBM per device.

v0:
```python
import jax
import jax.numpy as jnp
from jax import lax
from jax.sharding import PartitionSpec as P

PARTNERS = 6
BF = jnp.bfloat16
F32 = jnp.float32


def one_hot(condition):
    return condition.astype(BF)


def dot(a, b, dims=((1,), (0,))):
    return lax.dot_general(a, b, (dims, ((), ())), preferred_element_type=F32)


def exchange(x):
    return lax.all_to_all(x, "blk", split_axis=0, concat_axis=0, tiled=True)


def per_device(
    features,
    row_target,
    tile_values,
    tile_rows,
    tile_cols,
    tile_counts,
    weight,
    layer_bias,
    out_grad,
):
    blocks = lax.axis_size("blk")
    members = lax.axis_size("rep")
    me = lax.axis_index("blk")
    member = lax.axis_index("rep")
    rows, cols = features.shape
    slots, tile = tile_values.shape[2:4]
    tiles = rows // tile
    bucket = 2 * rows // blocks
    piece = rows // blocks
    full_weight = lax.all_gather(weight, "rep", axis=0, tiled=True)
    all_counts = lax.all_gather(tile_counts[0], "blk", axis=0).reshape(blocks, blocks)
    ids = jnp.arange(blocks, dtype=jnp.int32)
    target = row_target // rows
    landing = row_target % rows
    hits = target[None, :] == ids[:, None]
    at = jnp.arange(rows, dtype=jnp.int32)
    earlier = dot(one_hot(hits), one_hot(at[:, None] < at[None, :]))
    rank = jnp.sum(jnp.where(hits, earlier, 0.0), axis=0).astype(jnp.int32)
    slot = target * bucket + rank
    to_slot = slot[None, :] == jnp.arange(blocks * bucket, dtype=jnp.int32)[:, None]
    send_rows = dot(one_hot(to_slot), features).astype(BF)
    send_where = jnp.sum(jnp.where(to_slot, landing[None, :] + 1, 0), axis=1) - 1
    got_rows = exchange(send_rows.reshape(blocks, bucket, cols)).reshape(-1, cols)
    got_where = exchange(send_where.reshape(blocks, bucket)).reshape(-1)
    regrouped = dot(one_hot(got_where[None, :] == at[:, None]), got_rows).astype(BF)
    partner = (all_counts > 0) & (ids[:, None] != ids[None, :])
    order = dot(one_hot(partner), one_hot(ids[:, None] < ids[None, :]))
    wanted = jnp.arange(PARTNERS, dtype=F32)
    choose = partner[:, None, :] & (order[:, None, :] == wanted[None, :, None])
    flat_choose = one_hot(choose).reshape(blocks * PARTNERS, blocks)
    mine = lax.dynamic_index_in_dim(choose, me, 0, keepdims=False)
    mine = jnp.concatenate([mine, (ids == me)[None]], axis=0).astype(jnp.int32)
    which = jnp.sum(mine * ids[None, :], axis=1)
    meets = PARTNERS + 1
    row_of = jnp.sum(mine[:, :, None] * tile_rows[0][None], axis=1)
    col_of = jnp.sum(mine[:, :, None] * tile_cols[0][None], axis=1)
    live = jnp.sum(mine * tile_counts[0][None], axis=1)
    live = jnp.arange(slots, dtype=jnp.int32)[None, :] < live[:, None]
    tile_ids = jnp.arange(tiles, dtype=jnp.int32)
    spot = (
        live[:, :, None, None]
        & (row_of[:, :, None, None] == tile_ids[None, None, :, None])
        & (col_of[:, :, None, None] == tile_ids[None, None, None, :])
    )
    adjacency = []
    for k in range(meets):
        values = lax.dynamic_index_in_dim(tile_values[0], which[k], 0, keepdims=False)
        dense = jnp.zeros((tiles, tile, tiles, tile), BF)
        for s in range(slots):
            dense = jnp.where(spot[k, s][:, None, :, None], values[s][None, :, None, :], dense)
        adjacency.append(dense.reshape(rows, rows))
    adjacency = jnp.concatenate(adjacency, axis=1)
    spread = exchange(regrouped.reshape(blocks, piece, cols)).reshape(blocks, piece * cols)
    served = dot(flat_choose, spread).astype(BF)
    served = exchange(served.reshape(blocks, PARTNERS * piece, cols))
    served = served.reshape(blocks, PARTNERS, piece, cols).transpose(1, 0, 2, 3)
    inputs = jnp.concatenate([served.reshape(PARTNERS * rows, cols), regrouped], axis=0)
    mixed = dot(adjacency, inputs).astype(BF)
    full_mixed = lax.all_gather(mixed, "rep", axis=1, tiled=True)
    pre = dot(full_mixed, full_weight) + layer_bias
    sigma = jax.nn.sigmoid(pre)
    share = rows // members
    output = lax.dynamic_slice_in_dim((pre * sigma).astype(BF), member * share, share, 0)
    pre_grad = (out_grad.astype(F32) * sigma * (1.0 + pre * (1.0 - sigma))).astype(BF)
    mixed_grad = dot(pre_grad, weight, ((1,), (1,))).astype(BF)
    terms = dot(adjacency, mixed_grad, ((0,), (0,)))
    own = terms[PARTNERS * rows :]
    away = terms[: PARTNERS * rows].astype(BF).reshape(PARTNERS, blocks, piece, cols)
    away = exchange(away.transpose(1, 0, 2, 3).reshape(blocks, PARTNERS * piece, cols))
    away = away.reshape(blocks * PARTNERS, piece * cols)
    summed = dot(flat_choose, away, ((0,), (0,)))
    back = exchange(summed.reshape(blocks, piece, cols)).reshape(rows, cols)
    feature_grad = (back + own).astype(BF)
    weight_part = dot(mixed, pre_grad, ((0,), (0,)))
    bias_part = jnp.sum(pre_grad.astype(F32), axis=0)
    bias_grad = jnp.sum(lax.all_gather(bias_part, "blk", axis=0), axis=0)
    wide = weight_part.shape[1]
    weight_part = exchange(weight_part.reshape(blocks, -1, wide))
    weight_grad = lax.all_gather(jnp.sum(weight_part, axis=0), "blk", axis=0, tiled=True)
    return (output, weight_grad, bias_grad, feature_grad)


def solution(mesh):
    in_specs = (
        P("blk", "rep"),
        P("blk"),
        P("blk", None, None, None, None),
        P("blk", None, None),
        P("blk", None, None),
        P("blk", None),
        P("rep", None),
        P(),
        P("blk", None),
    )
    out_specs = (P(("blk", "rep"), None), P("rep", None), P(), P("blk", "rep"))
    return jax.shard_map(
        per_device, mesh=mesh, in_specs=in_specs, out_specs=out_specs, check_vma=False
    )
```

profile of v0, /device:TPU:32, one launch (start us, length us, event | category | flops | bytes accessed | tf_op | source)
XLA Modules:
  0.0 724.9 jit_solution(7916404086749864458)
XLA Ops:
  0.6 0.7 fusion.22
  1.9 0.7 sub.17
  2.6 14.2 %all-to-all-start = ((s32[64,1,16]{2,1,0:T(1,128)}), s32[64,1,16]{2,1,0:T(1,128)S(1)}, u32[]{:S(2)}, u32[]{:S(2)}) async-start(s32[64,1,16]{2,1,0:T(1,128)} %bitcast.70), calls=%async_computation | async-start | bytes 65536 | tf_op jit(solution)/shard_map/all_to_all | solution.py:20
  16.8 175.0 %all-gather.1 = s32[64,1,64]{2,1,0:T(1,128)S(1)} all-gather(s32[1,1,64]{2,1,0:T(1,128)} %bitcast.215), channel_id=1, replica_groups=mesh['blk'=64,'rep'=4] {'blk'}, dimensions={0}, use_global_device_ids=true | all-gather | bytes 16640 | tf_op jit(solution)/shard_map/all_gather | solution.py:44
  192.1 0.8 select_reduce_fusion.1
  202.6 1.0 multiply_reduce_fusion.1
  208.9 2.0 dynamic-slice_bitcast_fusion.3
  212.3 1.2 fusion.2
  213.5 11.2 %all-to-all-start.1 = ((bf16[64,16,128]{2,1,0:T(8,128)(2,1)}), bf16[64,16,128]{2,1,0:T(8,128)(2,1)}, u32[]{:S(2)}, u32[]{:S(2)}) async-start(bf16[64,16,128]{2,1,0:T(8,128)(2,1)} %bitcast.71), calls=%async_computation.1 | async-start | bytes 524288 | tf_op jit(solution)/shard_map/all_to_all | solution.py:20
  225.5 1.3 select_select_fusion.1
  227.3 1.5 reduce.4
  228.9 9.0 %all-to-all-done.1 = bf16[64,16,128]{2,1,0:T(8,128)(2,1)} async-done(((bf16[64,16,128]{2,1,0:T(8,128)(2,1)}), bf16[64,16,128]{2,1,0:T(8,128)(2,1)}, u32[]{:S(2)}, u32[]{:S(2)}) %all-to-all-start.1) | async-done | bytes 262176 | tf_op jit(solution)/shard_map/all_to_all | solution.py:20
  237.9 2.1 fusion.3
  240.0 5.7 all-to-all-start.2
  245.7 1.2 select_select_fusion
  247.6 0.9 bitcast_dynamic-update-slice_fusion.6
  248.5 9.1 %all-to-all-done.2 = bf16[64,8,128]{2,1,0:T(8,128)(2,1)} async-done(((bf16[64,8,128]{2,1,0:T(8,128)(2,1)}), bf16[64,8,128]{2,1,0:T(8,128)(2,1)}, u32[]{:S(2)}, u32[]{:S(2)}) %all-to-all-start.2) | async-done | bytes 131104 | tf_op jit(solution)/shard_map/all_to_all | solution.py:20
  257.7 1.3 convolution_convert_fusion
  259.0 1.2 reshape.423
  260.2 5.3 all-to-all-start.3
  265.4 8.0 %all_gather.20 = bf16[512,512]{1,0:T(8,128)(2,1)} all-gather(bf16[128,512]{1,0:T(8,128)(2,1)} %param.15), channel_id=1, replica_groups=mesh['blk'=64,'rep'=4] {'rep'}, dimensions={0}, use_global_device_ids=true | all-gather | bytes 655360 | tf_op jit(solution)/shard_map/all_gather | solution.py:43
  273.4 0.9 bitcast_dynamic-update-slice_fusion.5
  274.3 0.9 bitcast_dynamic-update-slice_fusion.4
  275.2 0.9 bitcast_dynamic-update-slice_fusion.3
  276.1 0.9 bitcast_dynamic-update-slice_fusion.2
  277.0 0.9 bitcast_dynamic-update-slice_fusion.1
  277.9 0.9 bitcast_dynamic-update-slice_fusion
  278.8 4.9 all-to-all-done.3
  283.9 3.2 convolution_convert_fusion.2
  287.1 6.5 all_gather.19
  293.7 2.1 convert_reduce_fusion
  295.8 3.6 fusion.4
  299.5 1.0 copy.73
  300.5 11.0 %all-to-all-start.5 = ((bf16[64,48,128]{2,1,0:T(8,128)(2,1)}), bf16[64,48,128]{2,1,0:T(8,128)(2,1)S(1)}, u32[]{:S(2)}, u32[]{:S(2)}) async-start(bf16[64,48,128]{2,1,0:T(8,128)(2,1)} %bitcast.198), calls=%async_computation.5 | async-start | bytes 1572864 | tf_op jit(solution)/shard_map/all_to_all | solution.py:20
  311.5 1.2 fusion.30
  312.6 0.9 reshape.426
  313.5 23.8 %all-to-all-done.5 = bf16[64,48,128]{2,1,0:T(8,128)(2,1)S(1)} async-done(((bf16[64,48,128]{2,1,0:T(8,128)(2,1)}), bf16[64,48,128]{2,1,0:T(8,128)(2,1)S(1)}, u32[]{:S(2)}, u32[]{:S(2)}) %all-to-all-start.5) | async-done | bytes 786464 | tf_op jit(solution)/shard_map/all_to_all | solution.py:20
  337.3 5.8 all-to-all-start.4
  343.8 1.2 fusion.28
  345.0 0.9 copy.50
  345.8 11.0 %all-to-all-done.4 = f32[64,2,512]{2,1,0:T(2,128)} async-done(((f32[64,2,512]{2,1,0:T(2,128)}), f32[64,2,512]{2,1,0:T(2,128)}, u32[]{:S(2)}, u32[]{:S(2)}) %all-to-all-start.4) | async-done | bytes 262176 | tf_op jit(solution)/shard_map/all_to_all | solution.py:20
  356.8 5.1 all-to-all-start.6
  361.9 176.7 %all-gather.3 = f32[64,1,512]{2,1,0:T(1,128)S(1)} all-gather(f32[1,1,512]{2,1,0:T(1,128)S(1)} %bitcast.214), channel_id=2, replica_groups=mesh['blk'=64,'rep'=4] {'blk'}, dimensions={0}, use_global_device_ids=true | all-gather | bytes 133120 | tf_op jit(solution)/shard_map/all_gather | solution.py:109
  538.6 0.7 reduce_sum.89
  539.3 1.7 fusion.12
  541.0 1.1 reduce_sum.87
  542.1 181.3 %all-gather.2 = f32[64,2,512]{2,1,0:T(2,128)S(1)} all-gather(f32[1,2,512]{2,1,0:T(2,128)S(1)} %bitcast.213), channel_id=1, replica_groups=mesh['blk'=64,'rep'=4] {'blk'}, dimensions={0}, use_global_device_ids=true | all-gather | bytes 266240 | tf_op jit(solution)/shard_map/all_gather | solution.py:112
  723.3 0.9 reshape.435
  (49 shorter events, 7.4 us)
Async XLA Ops:
  0.6 211.6 %copy-start = (bf16[512,128]{1,0:T(8,128)(2,1)S(1)}, bf16[512,128]{1,0:T(8,128)(2,1)}, u32[]{:S(2)}) copy-start(bf16[512,128]{1,0:T(8,128)(2,1)} %param.9) | copy-start | bytes 393220
  2.6 210.9 %all-to-all-start = ((s32[64,1,16]{2,1,0:T(1,128)}), s32[64,1,16]{2,1,0:T(1,128)S(1)}, u32[]{:S(2)}, u32[]{:S(2)}) async-start(s32[64,1,16]{2,1,0:T(1,128)} %bitcast.70), calls=%async_computation | async-start | bytes 65536 | tf_op jit(solution)/shard_map/all_to_all | solution.py:20
  213.5 11.2 %copy-start.6 = (s32[64,1,16]{2,1,0:T(1,128)}, s32[64,1,16]{2,1,0:T(1,128)S(1)}, u32[]{:S(2)}) copy-start(s32[64,1,16]{2,1,0:T(1,128)S(1)} %all-to-all-done) | copy-start | bytes 12292
  213.5 24.4 %all-to-all-start.1 = ((bf16[64,16,128]{2,1,0:T(8,128)(2,1)}), bf16[64,16,128]{2,1,0:T(8,128)(2,1)}, u32[]{:S(2)}, u32[]{:S(2)}) async-start(bf16[64,16,128]{2,1,0:T(8,128)(2,1)} %bitcast.71), calls=%async_computation.1 | async-start | bytes 524288 | tf_op jit(solution)/shard_map/all_to_all | solution.py:20
  240.0 17.7 %all-to-all-start.2 = ((bf16[64,8,128]{2,1,0:T(8,128)(2,1)}), bf16[64,8,128]{2,1,0:T(8,128)(2,1)}, u32[]{:S(2)}, u32[]{:S(2)}) async-start(bf16[64,8,128]{2,1,0:T(8,128)(2,1)} %bitcast.212), calls=%async_computation.2 | async-start | bytes 262144 | tf_op jit(solution)/shard_map/all_to_all | solution.py:20
  260.2 23.6 %all-to-all-start.3 = ((bf16[64,48,128]{2,1,0:T(8,128)(2,1)}), bf16[64,48,128]{2,1,0:T(8,128)(2,1)S(1)}, u32[]{:S(2)}, u32[]{:S(2)}) async-start(bf16[64,48,128]{2,1,0:T(8,128)(2,1)} %reshape.423), calls=%async_computation.3 | async-start | bytes 1572864 | tf_op jit(solution)/shard_map/all_to_all | solution.py:20
  265.4 12.4 %copy-start.1 = (bf16[4,128,4,128]{3,2,1,0:T(4,128)(2,1)S(1)}, bf16[4,128,4,128]{3,2,1,0:T(4,128)(2,1)}, u32[]{:S(2)}) copy-start(bf16[4,128,4,128]{3,2,1,0:T(4,128)(2,1)} %select_select_fusion) | copy-start | bytes 1572868
  274.3 9.6 %copy-start.5 = (bf16[512,128]{1,0:T(8,128)(2,1)S(1)}, bf16[512,128]{1,0:T(8,128)(2,1)}, u32[]{:S(2)}) copy-start(bf16[512,128]{1,0:T(8,128)(2,1)} %fusion.3) | copy-start | bytes 393220
  283.7 9.9 %copy-start.4 = (bf16[512,512]{1,0:T(8,128)(2,1)S(1)}, bf16[512,512]{1,0:T(8,128)(2,1)}, u32[]{:S(2)}) copy-start(bf16[512,512]{1,0:T(8,128)(2,1)} %all_gather.20) | copy-start | bytes 1572868
  283.7 9.9 %copy-start.7 = (bf16[512,512]{1,0:T(8,128)(2,1)S(1)}, bf16[512,512]{1,0:T(8,128)(2,1)}, u32[]{:S(2)}) copy-start(bf16[512,512]{1,0:T(8,128)(2,1)} %param.17) | copy-start | bytes 1572868
  283.7 9.9 %copy-start.8 = (f32[512]{0:T(512)S(1)}, f32[512]{0:T(512)}, u32[]{:S(2)}) copy-start(f32[512]{0:T(512)} %param.16) | copy-start | bytes 6148
  287.1 8.7 %copy-start.3 = (bf16[512,128]{1,0:T(8,128)(2,1)}, bf16[512,128]{1,0:T(8,128)(2,1)S(1)}, u32[]{:S(2)}) copy-start(bf16[512,128]{1,0:T(8,128)(2,1)S(1)} %convolution_convert_fusion.2) | copy-start | bytes 393220
  293.7 2.1 copy-start.2
  300.5 36.8 %all-to-all-start.5 = ((bf16[64,48,128]{2,1,0:T(8,128)(2,1)}), bf16[64,48,128]{2,1,0:T(8,128)(2,1)S(1)}, u32[]{:S(2)}, u32[]{:S(2)}) async-start(bf16[64,48,128]{2,1,0:T(8,128)(2,1)} %bitcast.198), calls=%async_computation.5 | async-start | bytes 1572864 | tf_op jit(solution)/shard_map/all_to_all | solution.py:20
  337.3 19.5 %all-to-all-start.4 = ((f32[64,2,512]{2,1,0:T(2,128)}), f32[64,2,512]{2,1,0:T(2,128)}, u32[]{:S(2)}, u32[]{:S(2)}) async-start(f32[64,2,512]{2,1,0:T(2,128)} %reshape.426), calls=%async_computation.4 | async-start | bytes 524288 | tf_op jit(solution)/shard_map/all_to_all | solution.py:20
  356.8 367.4 %all-to-all-start.6 = ((f32[64,8,128]{2,1,0:T(8,128)}), f32[64,8,128]{2,1,0:T(8,128)S(1)}, u32[]{:S(2)}, u32[]{:S(2)}) async-start(f32[64,8,128]{2,1,0:T(8,128)} %copy.50), calls=%async_computation.6 | async-start | bytes 524288 | tf_op jit(solution)/shard_map/all_to_all | solution.py:20
where the time goes:
time: 726 us; the launch traced here: 725 us
  blocking collectives  547 us (75%)
  starting transfers between devices  58.2 us (8%)
  waiting for transfers between devices  57.9 us (8%)
  local copies, waits for them, and re-layouts  17.3 us (2%)
  matrix products  16.1 us (2%)
  between operations  14.3 us (2%)
  other arithmetic  13.6 us (2%)
    all_gather x1, blocking collectives, per_device(): lax.all_gather(jnp.sum(weight_part, axis=0), 'blk', axis=0, tiled=True)  181 us
    all_gather x1, blocking collectives, per_device(): bias_grad = jnp.sum(lax.all_gather(bias_part, 'blk', axis=0), axis=0)  177 us
    all_gather x1, blocking collectives, per_device(): lax.all_gather(tile_counts[0], 'blk', axis=0).reshape(blocks, blocks)  175 us
    all_to_all x7, starting transfers between devices, exchange(): return lax.all_to_all(x, 'blk', split_axis=0, concat_axis=0, tiled=True)  58.2 us
    all_to_all x7, waiting for transfers between devices, exchange(): return lax.all_to_all(x, 'blk', split_axis=0, concat_axis=0, tiled=True)  57.9 us
    dot_general x10, matrix products, dot(): return lax.dot_general(a, b, (dims, ((), ())), preferred_element_type=F32)  16.1 us
  transfers between devices with their start and end apart: 7, of which 5 were waited for; matrix products, arithmetic and copies ran while one was open for 4% of the time, Pallas kernels for 0%

commit v1 on v0

--- a/solution.py
+++ b/solution.py
@@ -109,7 +109,12 @@
     bias_grad = jnp.sum(lax.all_gather(bias_part, "blk", axis=0), axis=0)
     wide = weight_part.shape[1]
     weight_part = exchange(weight_part.reshape(blocks, -1, wide))
-    weight_grad = lax.all_gather(jnp.sum(weight_part, axis=0), "blk", axis=0, tiled=True)
+    weight_grad = jnp.concatenate(
+        lax.all_to_all(
+            jnp.stack([jnp.sum(weight_part, axis=0)] * lax.axis_size("blk")), "blk", 0, 0
+        ),
+        axis=0,
+    )
     return (output, weight_grad, bias_grad, feature_grad)
 
 

time: 726 us -> 566 us (0.78)
  blocking collectives: 547 us -> 366 us
  waiting for transfers between devices: 57.9 us -> 68.5 us
    all_gather x1 -> x0, blocking collectives: 181 us -> none  [per_device(): lax.all_gather(jnp.sum(weight_part, axis=0), 'blk', axis=0, tiled=True)]
    all_to_all x0 -> x1, waiting for transfers between devices: none -> 10.5 us  [per_device(): lax.all_to_all(jnp.stack([jnp.sum(weight_part, axis=0)] * lax.axis_size('...]
  transfers between devices with their start and end apart: 7 -> 8, of which waited for: 5 -> 6; matrix products, arithmetic and copies ran while one was open for 4% -> 6% of each run, Pallas kernels for 0% -> 0%
where the time goes in v1:
time: 566 us; the launch traced here: 559 us
  blocking collectives  366 us (65%)
  waiting for transfers between devices  68.5 us (12%)
  starting transfers between devices  63.5 us (11%)
  local copies, waits for them, and re-layouts  19 us (3%)
  matrix products  15.2 us (3%)
  between operations  14.3 us (3%)
  other arithmetic  12.6 us (2%)
    all_gather x1, blocking collectives, per_device(): bias_grad = jnp.sum(lax.all_gather(bias_part, 'blk', axis=0), axis=0)  176 us
    all_gather x1, blocking collectives, per_device(): lax.all_gather(tile_counts[0], 'blk', axis=0).reshape(blocks, blocks)  175 us
    all_to_all x7, waiting for transfers between devices, exchange(): return lax.all_to_all(x, 'blk', split_axis=0, concat_axis=0, tiled=True)  58.1 us
    all_to_all x7, starting transfers between devices, exchange(): return lax.all_to_all(x, 'blk', split_axis=0, concat_axis=0, tiled=True)  57.6 us
    dot_general x10, matrix products, dot(): return lax.dot_general(a, b, (dims, ((), ())), preferred_element_type=F32)  15.2 us
  transfers between devices with their start and end apart: 8, of which 6 were waited for; matrix products, arithmetic and copies ran while one was open for 6% of the time, Pallas kernels for 0%

profile of v1, /device:TPU:32, one launch (start us, length us, event | category | flops | bytes accessed | tf_op | source)
XLA Modules:
  0.0 559.2 jit_solution(1920977353587183758)
XLA Ops:
  0.6 0.7 fusion.22
  1.9 0.7 sub.17
  2.6 14.2 %all-to-all-start = ((s32[64,1,16]{2,1,0:T(1,128)}), s32[64,1,16]{2,1,0:T(1,128)S(1)}, u32[]{:S(2)}, u32[]{:S(2)}) async-start(s32[64,1,16]{2,1,0:T(1,128)} %bitcast.70), calls=%async_computation | async-start | bytes 65536 | tf_op jit(solution)/shard_map/all_to_all | solution.py:20
  16.8 175.0 %all-gather.1 = s32[64,1,64]{2,1,0:T(1,128)S(1)} all-gather(s32[1,1,64]{2,1,0:T(1,128)} %bitcast.213), channel_id=1, replica_groups=mesh['blk'=64,'rep'=4] {'blk'}, dimensions={0}, use_global_device_ids=true | all-gather | bytes 16640 | tf_op jit(solution)/shard_map/all_gather | solution.py:44
  192.1 0.8 select_reduce_fusion.1
  202.6 1.0 multiply_reduce_fusion.1
  208.9 2.0 dynamic-slice_bitcast_fusion.3
  212.3 1.2 fusion.2
  213.5 11.2 %all-to-all-start.1 = ((bf16[64,16,128]{2,1,0:T(8,128)(2,1)}), bf16[64,16,128]{2,1,0:T(8,128)(2,1)}, u32[]{:S(2)}, u32[]{:S(2)}) async-start(bf16[64,16,128]{2,1,0:T(8,128)(2,1)} %bitcast.71), calls=%async_computation.1 | async-start | bytes 524288 | tf_op jit(solution)/shard_map/all_to_all | solution.py:20
  225.5 1.3 select_select_fusion.1
  227.3 1.5 reduce.4
  228.9 9.0 %all-to-all-done.1 = bf16[64,16,128]{2,1,0:T(8,128)(2,1)} async-done(((bf16[64,16,128]{2,1,0:T(8,128)(2,1)}), bf16[64,16,128]{2,1,0:T(8,128)(2,1)}, u32[]{:S(2)}, u32[]{:S(2)}) %all-to-all-start.1) | async-done | bytes 262176 | tf_op jit(solution)/shard_map/all_to_all | solution.py:20
  237.9 2.1 fusion.3
  240.0 5.7 %all-to-all-start.2 = ((bf16[64,8,128]{2,1,0:T(8,128)(2,1)}), bf16[64,8,128]{2,1,0:T(8,128)(2,1)}, u32[]{:S(2)}, u32[]{:S(2)}) async-start(bf16[64,8,128]{2,1,0:T(8,128)(2,1)} %bitcast.211), calls=%async_computation.2 | async-start | bytes 262144 | tf_op jit(solution)/shard_map/all_to_all | solution.py:20
  245.7 1.2 select_select_fusion
  247.6 0.9 bitcast_dynamic-update-slice_fusion.6
  248.5 9.1 %all-to-all-done.2 = bf16[64,8,128]{2,1,0:T(8,128)(2,1)} async-done(((bf16[64,8,128]{2,1,0:T(8,128)(2,1)}), bf16[64,8,128]{2,1,0:T(8,128)(2,1)}, u32[]{:S(2)}, u32[]{:S(2)}) %all-to-all-start.2) | async-done | bytes 131104 | tf_op jit(solution)/shard_map/all_to_all | solution.py:20
  257.7 1.3 convolution_convert_fusion
  259.0 1.2 reshape.428
  260.2 5.3 all-to-all-start.3
  265.4 8.0 %all_gather.17 = bf16[512,512]{1,0:T(8,128)(2,1)} all-gather(bf16[128,512]{1,0:T(8,128)(2,1)} %param.15), channel_id=1, replica_groups=mesh['blk'=64,'rep'=4] {'rep'}, dimensions={0}, use_global_device_ids=true | all-gather | bytes 655360 | tf_op jit(solution)/shard_map/all_gather | solution.py:43
  273.4 0.9 bitcast_dynamic-update-slice_fusion.5
  274.3 0.9 bitcast_dynamic-update-slice_fusion.4
  275.2 0.9 bitcast_dynamic-update-slice_fusion.3
  276.1 0.9 bitcast_dynamic-update-slice_fusion.2
  277.0 0.9 bitcast_dynamic-update-slice_fusion.1
  277.9 0.9 bitcast_dynamic-update-slice_fusion
  278.8 5.0 all-to-all-done.3
  283.9 3.2 convolution_convert_fusion.2
  287.1 6.5 %all_gather.16 = bf16[512,512]{1,0:T(8,128)(2,1)S(1)} all-gather(bf16[512,128]{1,0:T(8,128)(2,1)S(1)} %convolution_convert_fusion.2), channel_id=1, replica_groups=mesh['blk'=64,'rep'=4] {'rep'}, dimensions={1}, use_global_device_ids=true | all-gather | bytes 655360 | tf_op jit(solution)/shard_map/all_gather | solution.py:92
  293.7 2.1 convert_reduce_fusion
  296.0 0.9 reshape.431
  296.9 11.0 %all-to-all-start.4 = ((f32[64,2,512]{2,1,0:T(2,128)}), f32[64,2,512]{2,1,0:T(2,128)S(1)}, u32[]{:S(2)}, u32[]{:S(2)}) async-start(f32[64,2,512]{2,1,0:T(2,128)} %reshape.431), calls=%async_computation.4 | async-start | bytes 524288 | tf_op jit(solution)/shard_map/all_to_all | solution.py:20
  307.9 3.6 fusion.4
  311.5 1.0 copy.73
  312.6 10.3 %all-to-all-done.4 = f32[64,2,512]{2,1,0:T(2,128)S(1)} async-done(((f32[64,2,512]{2,1,0:T(2,128)}), f32[64,2,512]{2,1,0:T(2,128)S(1)}, u32[]{:S(2)}, u32[]{:S(2)}) %all-to-all-start.4) | async-done | bytes 262176 | tf_op jit(solution)/shard_map/all_to_all | solution.py:20
  322.9 5.1 all-to-all-start.6
  328.1 24.7 %all-to-all-done.6 = bf16[64,48,128]{2,1,0:T(8,128)(2,1)S(1)} async-done(((bf16[64,48,128]{2,1,0:T(8,128)(2,1)}), bf16[64,48,128]{2,1,0:T(8,128)(2,1)S(1)}, u32[]{:S(2)}, u32[]{:S(2)}) %all-to-all-start.6) | async-done | bytes 786464 | tf_op jit(solution)/shard_map/all_to_all | solution.py:20
  352.8 0.8 stack.2
  353.6 5.9 %all-to-all-start.5 = ((f32[64,2,512]{2,1,0:T(2,128)}), f32[64,2,512]{2,1,0:T(2,128)}, u32[]{:S(2)}, u32[]{:S(2)}) async-start(f32[64,2,512]{2,1,0:T(2,128)} %stack.2), calls=%async_computation.5 | async-start | bytes 524288 | tf_op jit(solution)/shard_map/all_to_all | solution.py:113
  360.1 1.2 fusion.28
  361.3 0.9 copy.50
  362.2 10.5 %all-to-all-done.5 = f32[64,2,512]{2,1,0:T(2,128)} async-done(((f32[64,2,512]{2,1,0:T(2,128)}), f32[64,2,512]{2,1,0:T(2,128)}, u32[]{:S(2)}, u32[]{:S(2)}) %all-to-all-start.5) | async-done | bytes 262176 | tf_op jit(solution)/shard_map/all_to_all | solution.py:113
  372.7 5.1 all-to-all-start.7
  377.8 176.5 %all-gather.2 = f32[64,1,512]{2,1,0:T(1,128)S(1)} all-gather(f32[1,1,512]{2,1,0:T(1,128)S(1)} %bitcast.212), channel_id=2, replica_groups=mesh['blk'=64,'rep'=4] {'blk'}, dimensions={0}, use_global_device_ids=true | all-gather | bytes 133120 | tf_op jit(solution)/shard_map/all_gather | solution.py:109
  554.3 0.7 reduce_sum.89
  555.0 1.7 fusion.12
  556.7 1.8 reshape.432
  (47 shorter events, 7.8 us)
Async XLA Ops:
  0.6 211.6 %copy-start = (bf16[512,128]{1,0:T(8,128)(2,1)S(1)}, bf16[512,128]{1,0:T(8,128)(2,1)}, u32[]{:S(2)}) copy-start(bf16[512,128]{1,0:T(8,128)(2,1)} %param.9) | copy-start | bytes 393220
  2.6 210.9 %all-to-all-start = ((s32[64,1,16]{2,1,0:T(1,128)}), s32[64,1,16]{2,1,0:T(1,128)S(1)}, u32[]{:S(2)}, u32[]{:S(2)}) async-start(s32[64,1,16]{2,1,0:T(1,128)} %bitcast.70), calls=%async_computation | async-start | bytes 65536 | tf_op jit(solution)/shard_map/all_to_all | solution.py:20
  213.5 11.2 %copy-start.4 = (s32[64,1,16]{2,1,0:T(1,128)}, s32[64,1,16]{2,1,0:T(1,128)S(1)}, u32[]{:S(2)}) copy-start(s32[64,1,16]{2,1,0:T(1,128)S(1)} %all-to-all-done) | copy-start | bytes 12292
  213.5 24.4 %all-to-all-start.1 = ((bf16[64,16,128]{2,1,0:T(8,128)(2,1)}), bf16[64,16,128]{2,1,0:T(8,128)(2,1)}, u32[]{:S(2)}, u32[]{:S(2)}) async-start(bf16[64,16,128]{2,1,0:T(8,128)(2,1)} %bitcast.71), calls=%async_computation.1 | async-start | bytes 524288 | tf_op jit(solution)/shard_map/all_to_all | solution.py:20
  240.0 17.7 %all-to-all-start.2 = ((bf16[64,8,128]{2,1,0:T(8,128)(2,1)}), bf16[64,8,128]{2,1,0:T(8,128)(2,1)}, u32[]{:S(2)}, u32[]{:S(2)}) async-start(bf16[64,8,128]{2,1,0:T(8,128)(2,1)} %bitcast.211), calls=%async_computation.2 | async-start | bytes 262144 | tf_op jit(solution)/shard_map/all_to_all | solution.py:20
  260.2 23.6 %all-to-all-start.3 = ((bf16[64,48,128]{2,1,0:T(8,128)(2,1)}), bf16[64,48,128]{2,1,0:T(8,128)(2,1)S(1)}, u32[]{:S(2)}, u32[]{:S(2)}) async-start(bf16[64,48,128]{2,1,0:T(8,128)(2,1)} %reshape.428), calls=%async_computation.3 | async-start | bytes 1572864 | tf_op jit(solution)/shard_map/all_to_all | solution.py:20
  265.4 12.4 %copy-start.1 = (bf16[4,128,4,128]{3,2,1,0:T(4,128)(2,1)S(1)}, bf16[4,128,4,128]{3,2,1,0:T(4,128)(2,1)}, u32[]{:S(2)}) copy-start(bf16[4,128,4,128]{3,2,1,0:T(4,128)(2,1)} %select_select_fusion) | copy-start | bytes 1572868
  283.7 9.9 %copy-start.3 = (bf16[512,512]{1,0:T(8,128)(2,1)S(1)}, bf16[512,512]{1,0:T(8,128)(2,1)}, u32[]{:S(2)}) copy-start(bf16[512,512]{1,0:T(8,128)(2,1)} %all_gather.17) | copy-start | bytes 1572868
  283.7 9.9 %copy-start.5 = (bf16[512,512]{1,0:T(8,128)(2,1)S(1)}, bf16[512,512]{1,0:T(8,128)(2,1)}, u32[]{:S(2)}) copy-start(bf16[512,512]{1,0:T(8,128)(2,1)} %param.17) | copy-start | bytes 1572868
  283.7 9.9 %copy-start.6 = (f32[512]{0:T(512)S(1)}, f32[512]{0:T(512)}, u32[]{:S(2)}) copy-start(f32[512]{0:T(512)} %param.16) | copy-start | bytes 6148
  293.7 14.2 %copy-start.2 = (bf16[128,512]{1,0:T(8,128)(2,1)S(1)}, bf16[128,512]{1,0:T(8,128)(2,1)}, u32[]{:S(2)}) copy-start(bf16[128,512]{1,0:T(8,128)(2,1)} %param.15) | copy-start | bytes 393220
  296.9 26.0 %all-to-all-start.4 = ((f32[64,2,512]{2,1,0:T(2,128)}), f32[64,2,512]{2,1,0:T(2,128)S(1)}, u32[]{:S(2)}, u32[]{:S(2)}) async-start(f32[64,2,512]{2,1,0:T(2,128)} %reshape.431), calls=%async_computation.4 | async-start | bytes 524288 | tf_op jit(solution)/shard_map/all_to_all | solution.py:20
  322.9 29.9 %all-to-all-start.6 = ((bf16[64,48,128]{2,1,0:T(8,128)(2,1)}), bf16[64,48,128]{2,1,0:T(8,128)(2,1)S(1)}, u32[]{:S(2)}, u32[]{:S(2)}) async-start(bf16[64,48,128]{2,1,0:T(8,128)(2,1)} %bitcast.197), calls=%async_computation.6 | async-start | bytes 1572864 | tf_op jit(solution)/shard_map/all_to_all | solution.py:20
  353.6 19.1 %all-to-all-start.5 = ((f32[64,2,512]{2,1,0:T(2,128)}), f32[64,2,512]{2,1,0:T(2,128)}, u32[]{:S(2)}, u32[]{:S(2)}) async-start(f32[64,2,512]{2,1,0:T(2,128)} %stack.2), calls=%async_computation.5 | async-start | bytes 524288 | tf_op jit(solution)/shard_map/all_to_all | solution.py:113
  372.7 185.9 %all-to-all-start.7 = ((f32[64,8,128]{2,1,0:T(8,128)}), f32[64,8,128]{2,1,0:T(8,128)S(1)}, u32[]{:S(2)}, u32[]{:S(2)}) async-start(f32[64,8,128]{2,1,0:T(8,128)} %copy.50), calls=%async_computation.7 | async-start | bytes 524288 | tf_op jit(solution)/shard_map/all_to_all | solution.py:20
